TPU v7x, 32 devices: a whole 2x2x4 slice. The times are simulated.
32 devices in a mesh: dom: 8 (over y, x, core), rep: 4 (over z).
Axes of the slice: x: 2, y: 2, z: 4, core: 2. Of those that a mesh axis runs over, the one named last changes fastest.
Arguments:
- features: float32 [2048, 256], P('dom'), may hold values from -6 to 6
- tile_values: bfloat16 [8, 64, 128, 128], P('dom', 'rep'), may hold values from 0 to 0.03125
- tile_rows: int32 [8, 64], P('dom', 'rep'), may hold values from 0 to 1
- tile_cols: int32 [8, 64], P('dom', 'rep'), may hold values from 0 to 15, as said below
- weight: float32 [256, 256], replicated, may hold values from -0.375 to 0.375
- bias: float32 [256], replicated, may hold values from -3 to 3
- cotangent: float32 [2048, 256], P('dom'), may hold values from -6 to 6
Outputs:
- activations: float32 [2048, 256], P('dom')
- grad_features: float32 [2048, 256], P('dom')
- grad_weight: float32 [256, 256], replicated
- grad_bias: float32 [256], replicated
Inputs may be any that keep to these rules, and one draw needn't show every extreme that they name: `tile_cols`: within each share of 16 consecutive tiles of a partition, every tile column 0 to 15 appears exactly once.
All inputs are finite; a program needn't handle non-finite values.
Results may differ from a plain program's by a relative error of at most 0.0003.
Values sent between devices are 32-bit elements; how exact they have to be, the bound alone decides.
A program may use at most 64 MiB of HBM per device.

v0:
```python
import jax
import jax.numpy as jnp
from jax import lax
from jax.sharding import PartitionSpec as P


def body(features, tile_values, tile_rows, tile_cols, weight, bias, cotangent):
    highest = lax.Precision.HIGHEST
    values = tile_values[0].astype(jnp.float32)
    row_ids = tile_rows[0]
    col_ids = tile_cols[0]
    tile_size = values.shape[1]
    node_rows = features.shape[0]
    feat_width = features.shape[1]
    row_blocks = node_rows // tile_size
    shard_piece = lax.all_gather(features, "dom", axis=0, tiled=True)
    block_count = shard_piece.shape[0] // tile_size
    blocks = shard_piece.reshape(block_count, tile_size, feat_width)
    offsets = col_ids[:, None]
    select = (offsets == jnp.arange(block_count, dtype=jnp.int32)[None, :]).astype(jnp.float32)
    selected = jnp.einsum("sn,nif->sif", select, blocks, precision=highest)
    products = jnp.einsum("sij,sjf->sif", values, selected, precision=highest)
    row_select = (row_ids[None, :] == jnp.arange(row_blocks, dtype=jnp.int32)[:, None]).astype(
        jnp.float32
    )
    partial_rows = jnp.einsum("bs,sif->bif", row_select, products, precision=highest).reshape(
        node_rows, feat_width
    )
    aggregated = lax.psum(partial_rows, "rep")
    before = jnp.dot(aggregated, weight, precision=highest) + bias
    gate_value = jax.nn.sigmoid(before)
    output = before * gate_value
    grad_pre = cotangent * gate_value * (1.0 + before * (1.0 - gate_value))
    messages = jnp.dot(grad_pre, weight.T, precision=highest)
    weight_term = jnp.dot(aggregated.T, grad_pre, precision=highest)
    activations, messages, weight_term, bias_term = (
        output,
        messages,
        weight_term,
        jnp.sum(grad_pre, axis=0),
    )
    grad_weight, grad_bias = lax.psum((weight_term, bias_term), "dom")
    message_blocks = messages.reshape(row_blocks, tile_size, feat_width)
    picked_messages = jnp.einsum("bs,bif->sif", row_select, message_blocks, precision=highest)
    returned = jnp.einsum("sji,sjf->sif", values, picked_messages, precision=highest)
    block_count = node_rows * lax.axis_size("dom") // tile_size
    offsets = col_ids[None, :]
    select = (offsets == jnp.arange(block_count, dtype=jnp.int32)[:, None]).astype(jnp.float32)
    source_part = lax.psum_scatter(
        jnp.einsum("ns,sif->nif", select, returned, precision=highest).reshape(
            node_rows * lax.axis_size("dom"), feat_width
        ),
        "dom",
        scatter_dimension=0,
        tiled=True,
    )
    grad_features = lax.psum(source_part, "rep")
    return (activations, grad_features, grad_weight, grad_bias)


def solution(mesh):
    return jax.shard_map(
        body,
        mesh=mesh,
        in_specs=(
            P("dom", None),
            P("dom", "rep", None, None),
            P("dom", "rep"),
            P("dom", "rep"),
            P(),
            P(),
            P("dom", None),
        ),
        out_specs=(P("dom", None), P("dom", None), P(), P()),
        check_vma=False,
    )
```

profile of v0, /device:TPU:0, one launch (start us, length us, event | category | flops | bytes accessed | tf_op | source)
XLA Modules:
  0.0 246.7 jit_solution(1948898299063535947)
XLA Ops:
  7.2 0.7 all-gather.2.cloned.1.call-update
  8.0 32.6 %all-gather.2.cloned.1.call-done = f32[2048,256]{1,0:T(8,128)} async-done(((f32[256,256]{1,0:T(8,128)}), f32[2048,256]{1,0:T(8,128)}) %all-gather.2.cloned.1.call-update) | async-done | bytes 2097168 | tf_op jit(solution)/shard_map/all_gather | solution.py:16
  40.5 3.9 %fusion.8 = f32[16,128,256]{2,0,1:T(8,128)S(1)} fusion(f32[16,128,256]{2,1,0:T(8,128)} %bitcast.35, s32[16]{0:T(128)} %bitcast.40), kind=kOutput, calls=%fused_computation.8 | convolution fusion | flops 100663552 | bytes 4194368 | tf_op jit(solution)/shard_map/sn,nif->sif/dot_general | solution.py:21
  44.5 4.1 %fusion.6 = f32[16,256,128]{2,1,0:T(8,128)} fusion(f32[16,128,256]{2,0,1:T(8,128)S(1)} %fusion.8, bf16[1,16,128,128]{3,2,1,0:T(8,128)(2,1)S(1)} %copy-done), kind=kOutput, calls=%fused_computation.6 | convolution fusion | flops 805306368 | bytes 4718592 | tf_op jit(solution)/shard_map/sij,sjf->sif/dot_general | solution.py:22
  48.5 2.2 copy.15
  50.8 0.8 fusion.2
  51.6 0.7 copy.11
  52.4 0.2 reduce-scatter.2.cloned.1.call-start
  52.6 35.2 %all-reduce.4.cloned.1.call-done = f32[256,256]{1,0:T(8,128)} async-done(((f32[256,256]{1,0:T(8,128)}), f32[256,256]{1,0:T(8,128)}) %all-reduce.4.cloned.1.call-update) | async-done | bytes 262160 | tf_op jit(solution)/shard_map/psum | solution.py:29
  87.9 2.1 fusion.25
  90.0 0.4 fusion.26
  90.4 1.1 fusion.12
  91.5 2.7 %fusion.4 = f32[16,256,128]{2,1,0:T(8,128)S(1)} fusion(f32[16,128,256]{2,0,1:T(8,128)S(1)} %fusion.12, bf16[1,16,128,128]{3,2,1,0:T(8,128)(2,1)S(1)} %copy-done), kind=kOutput, calls=%fused_computation.4 | convolution fusion | flops 805306368 | bytes 4718592 | tf_op jit(solution)/shard_map/sji,sjf->sif/dot_general | solution.py:45
  94.3 2.1 copy.18
  96.4 2.7 %fusion = f32[16,128,256]{2,0,1:T(8,128)S(1)} fusion(f32[16,256,128]{1,0,2:T(8,128)} %copy.18, s32[16]{0:T(128)S(1)} %bitcast.41), kind=kOutput, calls=%fused_computation | convolution fusion | flops 100663552 | bytes 4194368 | tf_op jit(solution)/shard_map/ns,sif->nif/dot_general | solution.py:50
  99.1 2.6 %copy.12 = f32[16,128,256]{2,1,0:T(8,128)} copy(f32[16,128,256]{2,0,1:T(8,128)S(1)} %fusion) | data formatting | bytes 4194304 | tf_op jit(solution)/shard_map/ns,sif->nif/dot_general | solution.py:50
  101.7 0.9 copy-done.2
  102.6 1.3 fusion.27
  103.9 38.8 %reduce-scatter.2.cloned.1.call-done = f32[256,256]{1,0:T(8,128)} async-done(((f32[2048,256]{1,0:T(8,128)}), f32[256,256]{1,0:T(8,128)}) %reduce-scatter.2.cloned.1.call-update) | async-done | bytes 262160 | tf_op jit(solution)/shard_map/reduce_scatter | solution.py:49
  142.8 13.2 %psum.31 = f32[256]{0:T(256)} all-reduce(f32[256]{0:T(256)S(1)} %get-tuple-element.4), channel_id=1, replica_groups=mesh['dom'=8,'rep'=4] {'dom'}, use_global_device_ids=true, to_apply=%region_5.0 | all-reduce | flops 256 | bytes 2048 | tf_op jit(solution)/shard_map/psum | solution.py:42
  156.0 43.8 %all-reduce.8.cloned.1.call-done = f32[256,256]{1,0:T(8,128)} async-done(((f32[256,256]{1,0:T(8,128)}), f32[256,256]{1,0:T(8,128)}) %all-reduce.8.cloned.1.call-update) | async-done | bytes 262160 | tf_op jit(solution)/shard_map/psum | solution.py:42
  199.8 37.0 %all-reduce.6.cloned.1.call-done = f32[256,256]{1,0:T(8,128)} async-done(((f32[256,256]{1,0:T(8,128)}), f32[256,256]{1,0:T(8,128)}) %all-reduce.6.cloned.1.call-update) | async-done | bytes 262160 | tf_op jit(solution)/shard_map/psum | solution.py:57
  236.8 1.7 copy.30
  238.5 1.7 copy.31
  (21 shorter events, 0.3 us)
Async XLA Ops:
  7.2 37.3 %copy-start = (bf16[1,16,128,128]{3,2,1,0:T(8,128)(2,1)S(1)}, bf16[1,16,128,128]{3,2,1,0:T(8,128)(2,1)}, u32[]{:S(2)}) copy-start(bf16[1,16,128,128]{3,2,1,0:T(8,128)(2,1)} %param.8) | copy-start | bytes 1572868
  7.2 33.4 %all-gather.2.cloned.1.call-start = ((), (), s32[]{:S(2)}) async-start(), calls=%async_computation.1 | async-start | bytes 2359296 | tf_op jit(solution)/shard_map/all_gather | solution.py:16
  7.9 79.9 %all-reduce.4.cloned.1.call-start = ((), (), s32[]{:S(2)}) async-start(), calls=%async_computation.2 | async-start | bytes 524288 | tf_op jit(solution)/shard_map/psum | solution.py:29
  48.5 2.3 copy-start.3
  50.8 37.1 %copy-start.1 = (f32[256,256]{1,0:T(8,128)S(1)}, f32[256,256]{1,0:T(8,128)}, u32[]{:S(2)}) copy-start(f32[256,256]{1,0:T(8,128)} %param.11) | copy-start | bytes 786436
  50.8 37.0 %copy-start.5 = (f32[256,256]{1,0:T(8,128)S(1)}, f32[256,256]{1,0:T(8,128)}, u32[]{:S(2)}) copy-start(f32[256,256]{1,0:T(8,128)} %param.13) | copy-start | bytes 786436
  50.8 37.0 %copy-start.6 = (f32[256]{0:T(256)S(1)}, f32[256]{0:T(256)}, u32[]{:S(2)}) copy-start(f32[256]{0:T(256)} %param.12) | copy-start | bytes 3076
  52.4 90.4 %reduce-scatter.2.cloned.1.call-start = ((), (), s32[]{:S(2)}) async-start(), calls=%async_computation.3 | async-start | bytes 2359296 | tf_op jit(solution)/shard_map/reduce_scatter | solution.py:49
  94.3 2.1 copy-start.4
  101.6 0.9 copy-start.2
  101.6 98.2 %all-reduce.8.cloned.1.call-start = ((), (), s32[]{:S(2)}) async-start(), calls=%async_computation.5 | async-start | bytes 524288 | tf_op jit(solution)/shard_map/psum | solution.py:42
  103.9 132.9 %all-reduce.6.cloned.1.call-start = ((), (), s32[]{:S(2)}) async-start(), calls=%async_computation.4 | async-start | bytes 524288 | tf_op jit(solution)/shard_map/psum | solution.py:57
Sparse Core Ops, SparseCore 0:
  9.9 30.5 all-gather.1
  52.5 35.2 all-reduce.3
  101.8 40.9 reduce-scatter.1
  146.2 53.5 all-reduce.7
  202.1 34.6 all-reduce.5
where the time goes:
time: 247 us
  waiting for transfers between devices  188 us (76%)
  matrix products  19.2 us (8%)
  between operations  13.9 us (6%)
  blocking collectives  13.2 us (5%)
  local copies, waits for them, and re-layouts  11.8 us (5%)
    psum x1, waiting for transfers between devices, body(): grad_weight, grad_bias = lax.psum((weight_term, bias_term), 'dom')  43.8 us
    reduce_scatter x1, waiting for transfers between devices, body(): lax.psum_scatter(jnp.einsum('ns,sif->nif', select, returned, precision=hi...  38.8 us
    psum x1, waiting for transfers between devices, body(): grad_features = lax.psum(source_part, 'rep')  37 us
    psum x1, waiting for transfers between devices, body(): aggregated = lax.psum(partial_rows, 'rep')  35.2 us
    all_gather x1, waiting for transfers between devices, body(): shard_piece = lax.all_gather(features, 'dom', axis=0, tiled=True)  32.6 us
    psum x1, blocking collectives, body(): grad_weight, grad_bias = lax.psum((weight_term, bias_term), 'dom')  13.2 us
  transfers between devices with their start and end apart: 5, of which 5 were waited for; matrix products, arithmetic and copies ran while one was open for 1% of the time, Pallas kernels for 0%

commit v1 on v0

v1 whole, which is shorter than its diff:
```python
import functools

import jax
import jax.numpy as jnp
from jax import lax
from jax.experimental import pallas as pl
from jax.experimental.pallas import tpu as pltpu
from jax.sharding import PartitionSpec as P

F32 = jnp.float32
BF16 = jnp.bfloat16


def split(x):
    high = x.astype(BF16)
    return high, (x - high.astype(F32)).astype(BF16)


def mm(a, b, dims=((1,), (0,))):
    return lax.dot_general(a, b, (dims, ((), ())), preferred_element_type=F32)


def mm3(a, b, dims=((1,), (0,))):
    return mm(a[0], b[0], dims) + (mm(a[0], b[1], dims) + mm(a[1], b[0], dims))


def kernel(
    D, R, K,
    rows_ref, cols_ref, feat_ref, tiles_ref, weight_ref, bias_ref, cot_ref,
    act_ref, gfeat_ref, gweight_ref, gbias_ref,
    adj, adj_t, fbuf, part, rsbuf, agg, wterm, w1s, w1r, w2b, w3b,
    psend, precv, csend, crecv, srcp, rs2, gbuf,
    a_s, a_r, l_s, l_r, b_s, b_r, g_s, g_r,
    p_s, p_r, c_s, c_r, d_s, d_r, e_s, e_r,
    w1_s, w1_r, w2_s, w2_r, w3_s, w3_r,
):
    C = D // 2
    tile = tiles_ref.shape[2]
    slots = tiles_ref.shape[1]
    n_rows, feat = feat_ref.shape
    per = n_rows // tile
    half = feat // 2
    piece = w1s.shape[1] - 8
    d = lax.axis_index("dom")
    r = lax.axis_index("rep")
    chip, core = d // 2, d % 2
    other = 1 - core
    partner = chip * 2 + other

    def dom_at(k):
        return lax.rem(d + k, D)

    def rep_at(k):
        return lax.rem(r + k, R)

    def chip_at(k):
        return lax.rem(chip + k, C)

    def copy(src, dst, ss, rs, dom=None, rep=None):
        return pltpu.make_async_remote_copy(
            src_ref=src, dst_ref=dst, send_sem=ss, recv_sem=rs,
            device_id={"dom": d if dom is None else dom, "rep": r if rep is None else rep},
            device_id_type=pl.DeviceIdType.MESH,
        )

    sent = []

    def send(*args, **kw):
        c = copy(*args, **kw)
        c.start()
        sent.append(c)
        return c

    barrier = pltpu.get_barrier_semaphore()
    for k in range(1, D):
        pl.semaphore_signal(barrier, inc=1, device_id={"dom": dom_at(k), "rep": r}, device_id_type=pl.DeviceIdType.MESH)
    for k in range(1, R):
        pl.semaphore_signal(barrier, inc=1, device_id={"dom": d, "rep": rep_at(k)}, device_id_type=pl.DeviceIdType.MESH)
    pl.semaphore_wait(barrier, D - 1 + R - 1)

    lanes = [pl.ds(h * half, half) for h in range(2)]
    gather = {}
    relay = {}
    for h in range(2):
        own = feat_ref.at[:, lanes[h]]
        relay[h, 0] = send(own, fbuf.at[h, 0, 1], l_s.at[h, 0], l_r.at[h, 0], dom=partner)
        for k in range(1, C):
            gather[h, k] = send(own, fbuf.at[h, k, 0], a_s.at[h, k], a_r.at[h, k], dom=chip_at(k) * 2 + core)

    def place(q, carry):
        for j in range(per):
            col = q * per + j
            slot = jnp.int32(0)
            for s in range(slots):
                slot = jnp.where(cols_ref[0, s] == col, jnp.int32(s), slot)
            row = rows_ref[0, slot]
            values = tiles_ref[0, slot].astype(F32)
            turned = values.T
            for b in range(per):
                keep = jnp.where(row == b, jnp.float32(1), jnp.float32(0))
                adj[q, pl.ds(b * tile, tile), pl.ds(j * tile, tile)] = (values * keep).astype(BF16)
                adj_t[q, pl.ds(j * tile, tile), pl.ds(b * tile, tile)] = (turned * keep).astype(BF16)
        return carry

    lax.fori_loop(0, D, place, 0)
    w = split(weight_ref[...])

    def product(matrix, block):
        high, low = split(block)
        both = mm(matrix, jnp.concatenate([high, low], axis=1))
        return both[:, :half] + both[:, half:]

    reduce_rows = n_rows // R

    def rep_reduce(h, source, buf, ss, rs):
        return [
            send(source.at[h, rep_at(k)], buf.at[h, k], ss.at[h, k], rs.at[h, k], rep=rep_at(k))
            for k in range(1, R)
        ]

    def rep_gather(h, copies, source, buf, out, ss, rs):
        total = source[h, r]
        for k in range(1, R):
            copies[k - 1].wait_recv()
            total = total + buf[h, k]
        out[h, r] = total
        return [send(out.at[h, r], out.at[h, r], ss.at[h, k], rs.at[h, k], rep=rep_at(k)) for k in range(1, R)]

    before = bias_ref[...]
    reduces = []
    gathers = []
    for h in range(2):
        total = product(adj[d], feat_ref[:, h * half:(h + 1) * half])
        relay[h, 0].wait_recv()
        total = total + product(adj[partner], fbuf[h, 0, 1])
        for k in range(1, C):
            gather[h, k].wait_recv()
            relay[h, k] = send(fbuf.at[h, k, 0], fbuf.at[h, k, 1], l_s.at[h, k], l_r.at[h, k], dom=partner)
            source = lax.rem(chip + C - k, C)
            total = total + product(adj[source * 2 + core], fbuf[h, k, 0])
        for k in range(1, C):
            source = lax.rem(chip + C - k, C)
            relay[h, k].wait_recv()
            total = total + product(adj[source * 2 + other], fbuf[h, k, 1])
        part[h] = total.reshape(R, reduce_rows, half)
        reduces.append(rep_reduce(h, part, rsbuf, b_s, b_r))
        if h == 0:
            gathers.append(rep_gather(0, reduces[0], part, rsbuf, agg, g_s, g_r))
    gathers.append(rep_gather(1, reduces[1], part, rsbuf, agg, g_s, g_r))

    sums = []
    for h in range(2):
        for c in gathers[h]:
            c.wait_recv()
        a = split(agg[h].reshape(n_rows, half))
        sums.append(a)
        before = before + mm3(a, (w[0][h * half:(h + 1) * half], w[1][h * half:(h + 1) * half]))
    gate = 1.0 / (1.0 + jnp.exp(-before))
    act_ref[...] = before * gate
    grad_pre = cot_ref[...] * gate * (1.0 + before * (1.0 - gate))
    g = split(grad_pre)

    scatters = []
    for h in range(2):
        m = mm3(g, (w[0][h * half:(h + 1) * half], w[1][h * half:(h + 1) * half]), ((1,), (1,)))
        high, low = split(m)
        both = jnp.concatenate([high, low], axis=1)

        def back(q):
            x = mm(adj_t[q], both)
            return x[:, :half] + x[:, half:]

        order = list(range(1, C)) + [0]
        pairs = {}
        for k in order:
            psend[h, k] = back(chip_at(k) * 2 + other)
            pairs[k] = send(psend.at[h, k], precv.at[h, k], p_s.at[h, k], p_r.at[h, k], dom=partner)
        chips = []
        for k in order:
            x = back(chip_at(k) * 2 + core)
            pairs[k].wait_recv()
            csend[h, k] = x + precv[h, k]
            if k:
                chips.append(
                    send(csend.at[h, k], crecv.at[h, k], c_s.at[h, k], c_r.at[h, k], dom=chip_at(k) * 2 + core)
                )
        scatters.append(chips)

        if h == 0:
            for b in range(2):
                term = mm3(sums[b], g, ((0,), (0,)))
                count = half // piece
                wterm[pl.ds(b * count, count)] = term.reshape(count, piece, feat)
            bias_term = jnp.broadcast_to(jnp.sum(grad_pre, axis=0, keepdims=True), (8, feat))
            for o in range(K):
                w1s[o, pl.ds(0, piece)] = wterm[r * K + o]
                w1s[o, pl.ds(piece, 8)] = bias_term
            ones = []
            for k in range(1, D):
                owner = dom_at(k)
                if K == D:
                    ones.append(send(w1s.at[owner], w1r.at[k], w1_s.at[k], w1_r.at[k], dom=owner))
                else:
                    owner_in = jnp.minimum(owner, K - 1)
                    c = copy(w1s.at[owner_in], w1r.at[k], w1_s.at[k], w1_r.at[k], dom=owner)
                    ones.append(c)

                    @pl.when(owner < K)
                    def _(c=c):
                        c.start()
                        c.wait_send()

    twos = [
        copy(w2b.at[jnp.minimum(d, K - 1)], w2b.at[jnp.minimum(d, K - 1)], w2_s.at[k], w2_r.at[k], dom=dom_at(k))
        for k in range(1, D)
    ]

    def own_piece():
        total = w1s[jnp.minimum(d, K - 1)]
        for k in range(1, D):
            ones[k - 1].wait_recv()
            total = total + w1r[k]
        w2b[jnp.minimum(d, K - 1)] = total
        for c in twos:
            c.start()

    if K == D:
        own_piece()
        sent.extend(twos)
    else:
        @pl.when(d < K)
        def _():
            own_piece()
            for c in twos:
                c.wait_send()

    def back_sum(h):
        total = csend[h, 0]
        for k in range(1, C):
            scatters[h][k - 1].wait_recv()
            total = total + crecv[h, k]
        srcp[h] = total.reshape(R, reduce_rows, half)
        return rep_reduce(h, srcp, rs2, d_s, d_r)

    first = back_sum(0)

    for k in range(1, D):
        source = lax.rem(d + D - k, D)
        if K == D:
            copy(w2b.at[source], w2b.at[source], w2_s.at[k], w2_r.at[k], dom=dom_at(k)).wait_recv()
        else:
            @pl.when(source < K)
            def _(k=k, source=source):
                s = jnp.minimum(source, K - 1)
                copy(w2b.at[s], w2b.at[s], w2_s.at[k], w2_r.at[k], dom=dom_at(k)).wait_recv()
    w3b[r] = w2b[:, :piece].reshape(K * piece, feat)
    threes = [send(w3b.at[r], w3b.at[r], w3_s.at[k], w3_r.at[k], rep=rep_at(k)) for k in range(1, R)]
    gbias_ref[...] = w2b[0, piece:piece + 1]

    ends = [rep_gather(0, first, srcp, rs2, gbuf, e_s, e_r)]
    second = back_sum(1)
    ends.append(rep_gather(1, second, srcp, rs2, gbuf, e_s, e_r))
    for c in threes:
        c.wait_recv()
    gweight_ref[...] = w3b[...].reshape(feat, feat)
    for h in range(2):
        for c in ends[h]:
            c.wait_recv()
        gfeat_ref[:, h * half:(h + 1) * half] = gbuf[h].reshape(n_rows, half)
    for c in sent:
        c.wait_send()


def body(D, R, features, tile_values, tile_rows, tile_cols, weight, bias, cotangent):
    n_rows, feat = features.shape
    half = feat // 2
    C = D // 2
    share = feat // R
    K = min(D, share // 8)
    piece = share // K
    chunk = n_rows // R
    vmem = pl.BlockSpec(memory_space=pltpu.VMEM)
    smem = pl.BlockSpec(memory_space=pltpu.SMEM)

    def sems(*shape):
        return pltpu.SemaphoreType.DMA(shape)

    out = pl.pallas_call(
        functools.partial(kernel, D, R, K),
        out_shape=(
            jax.ShapeDtypeStruct((n_rows, feat), F32),
            jax.ShapeDtypeStruct((n_rows, feat), F32),
            jax.ShapeDtypeStruct((feat, feat), F32),
            jax.ShapeDtypeStruct((1, feat), F32),
        ),
        in_specs=[smem, smem] + [vmem] * 5,
        out_specs=(vmem,) * 4,
        scratch_shapes=[
            pltpu.VMEM((D, n_rows, n_rows), BF16),
            pltpu.VMEM((D, n_rows, n_rows), BF16),
            pltpu.VMEM((2, C, 2, n_rows, half), F32),
            pltpu.VMEM((2, R, chunk, half), F32),
            pltpu.VMEM((2, R, chunk, half), F32),
            pltpu.VMEM((2, R, chunk, half), F32),
            pltpu.VMEM((R * K, piece, feat), F32),
            pltpu.VMEM((K, piece + 8, feat), F32),
            pltpu.VMEM((D, piece + 8, feat), F32),
            pltpu.VMEM((K, piece + 8, feat), F32),
            pltpu.VMEM((R, share, feat), F32),
            pltpu.VMEM((2, C, n_rows, half), F32),
            pltpu.VMEM((2, C, n_rows, half), F32),
            pltpu.VMEM((2, C, n_rows, half), F32),
            pltpu.VMEM((2, C, n_rows, half), F32),
            pltpu.VMEM((2, R, chunk, half), F32),
            pltpu.VMEM((2, R, chunk, half), F32),
            pltpu.VMEM((2, R, chunk, half), F32),
        ]
        + [sems(2, C)] * 4
        + [sems(2, R)] * 4
        + [sems(2, C)] * 4
        + [sems(2, R)] * 4
        + [sems(D)] * 4
        + [sems(R)] * 2,
        compiler_params=pltpu.CompilerParams(
            collective_id=0, has_side_effects=True, vmem_limit_bytes=56 * 1024 * 1024
        ),
        name="layer",
    )(tile_rows, tile_cols, features, tile_values, weight, bias.reshape(1, feat), cotangent)
    activations, grad_features, grad_weight, grad_bias = out
    return activations, grad_features, grad_weight, grad_bias.reshape(feat)


def solution(mesh):
    D, R = mesh.shape["dom"], mesh.shape["rep"]
    return jax.shard_map(
        functools.partial(body, D, R),
        mesh=mesh,
        in_specs=(
            P("dom", None),
            P("dom", "rep", None, None),
            P("dom", "rep"),
            P("dom", "rep"),
            P(),
            P(),
            P("dom", None),
        ),
        out_specs=(P("dom", None), P("dom", None), P(), P()),
        check_vma=False,
    )
```

time: 247 us -> 76.2 us (0.31)
  waiting for transfers between devices: 188 us -> 0 us
  Pallas kernels: 0 us -> 71.4 us
  matrix products: 19.2 us -> 0 us
  between operations: 13.9 us -> 0.65 us
  blocking collectives: 13.2 us -> 0 us
  local copies, waits for them, and re-layouts: 11.8 us -> 4.03 us
    psum x3 -> x0, waiting for transfers between devices: 116 us -> none  [the longest x1 43.8 us: body(): grad_weight, grad_bias = lax.psum((weight_term, bias_term), 'dom')]
    pallas_call x0 -> x1, Pallas kernels: none -> 71.4 us  [body(): pl.pallas_call(functools.partial(kernel, D, R, K), out_shape=(jax.ShapeDt...]
    reduce_scatter x1 -> x0, waiting for transfers between devices: 38.8 us -> none  [body(): lax.psum_scatter(jnp.einsum('ns,sif->nif', select, returned, precision=hi...]
    all_gather x1 -> x0, waiting for transfers between devices: 32.6 us -> none  [body(): shard_piece = lax.all_gather(features, 'dom', axis=0, tiled=True)]
    dot_general x9 -> x0, matrix products: 19.2 us -> none  [the longest x1 4.07 us: body(): products = jnp.einsum('sij,sjf->sif', values, selected, precision=highest)]
    psum x1 -> x0, blocking collectives: 13.2 us -> none  [body(): grad_weight, grad_bias = lax.psum((weight_term, bias_term), 'dom')]
    dot_general x4 -> x0, local copies, waits for them, and re-layouts: 7.59 us -> none  [the longest x1 2.56 us: body(): jnp.einsum('ns,sif->nif', select, returned, precision=highest)]
  transfers between devices with their start and end apart: 5 -> 0, of which waited for: 5 -> 0; matrix products, arithmetic and copies ran while one was open for 1% -> 0% of each run, Pallas kernels for 0% -> 0%
where the time goes in v1:
time: 76.2 us; the launch traced here: 76 us
  Pallas kernels  71.4 us (94%)
  local copies, waits for them, and re-layouts  4.03 us (5%)
    pallas_call x1, Pallas kernels, body(): pl.pallas_call(functools.partial(kernel, D, R, K), out_shape=(jax.ShapeDt...  71.4 us
    unnamed x10, local copies, waits for them, and re-layouts  4.03 us

profile of v1, /device:TPU:0, one launch (start us, length us, event | category | flops | bytes accessed | tf_op | source)
XLA Modules:
  0.0 76.0 jit_solution(6901727300626224164)
XLA Ops:
  0.6 71.4 %layer.1 = (f32[256,256]{1,0:T(8,128)}, f32[256,256]{1,0:T(8,128)}, f32[256,256]{1,0:T(8,128)}, f32[1,256]{1,0:T(1,128)}) custom-call(s32[1,16]{1,0:T(1,128)} %rows_ref.1, s32[1,16]{1,0:T(1,128)} %cols_ref.1, f32[256,256]{1,0:T(8,128)} %feat_ref.1, bf16[1,16,128,128]{3,2,1,0:T(8,128)(2,1)} %tiles_ref.1, f32[256,256]{1,0:T(8,128)} %weight_ref.1, ...), custom_call_target="tpu_custom_call" | custom-call | tf_op jit(solution)/shard_map/layer/pallas_call | solution.py:288
  72.0 0.0 copy-start.1
  72.0 1.7 %copy.15 = f32[256,256]{1,0:T(8,128)} copy(f32[256,256]{1,0:T(8,128)} %get-tuple-element.16) | data formatting | bytes 524288
  73.7 0.0 copy-done.1
  73.7 0.0 copy-start
  73.7 0.7 copy.16
  74.4 0.3 copy-done
  74.8 0.0 copy-start.2
  74.8 0.7 copy.17
  75.5 0.0 copy-done.2
  75.5 0.6 copy.18
Async XLA Ops:
  72.0 1.7 %copy-start.1 = (f32[256,256]{1,0:T(8,128)S(1)}, f32[256,256]{1,0:T(8,128)}, u32[]{:S(2)}) copy-start(f32[256,256]{1,0:T(8,128)} %get-tuple-element.17) | copy-start | bytes 786436
  73.7 1.0 %copy-start = (f32[256,256]{1,0:T(8,128)S(1)}, f32[256,256]{1,0:T(8,128)}, u32[]{:S(2)}) copy-start(f32[256,256]{1,0:T(8,128)} %get-tuple-element.18) | copy-start | bytes 786436
  74.8 0.7 copy-start.2

commit v2 on v1

--- a/solution.py
+++ b/solution.py
@@ -32,7 +32,7 @@
     psend, precv, csend, crecv, srcp, rs2, gbuf,
     a_s, a_r, l_s, l_r, b_s, b_r, g_s, g_r,
     p_s, p_r, c_s, c_r, d_s, d_r, e_s, e_r,
-    w1_s, w1_r, w2_s, w2_r, w3_s, w3_r,
+    w1_s, w1_r, w2_s, w2_r, w3_s, w3_r, w4_s, w4_r,
 ):
     C = D // 2
     tile = tiles_ref.shape[2]
@@ -85,7 +85,9 @@
         own = feat_ref.at[:, lanes[h]]
         relay[h, 0] = send(own, fbuf.at[h, 0, 1], l_s.at[h, 0], l_r.at[h, 0], dom=partner)
         for k in range(1, C):
-            gather[h, k] = send(own, fbuf.at[h, k, 0], a_s.at[h, k], a_r.at[h, k], dom=chip_at(k) * 2 + core)
+            gather[h, k] = copy(own, fbuf.at[h, k, 0], a_s.at[h, k], a_r.at[h, k], dom=chip_at(k) * 2 + core)
+    for k in range(1, C):
+        gather[0, k].start()
 
     def place(q, carry):
         for j in range(per):
@@ -104,6 +106,10 @@
 
     lax.fori_loop(0, D, place, 0)
     w = split(weight_ref[...])
+    for k in range(1, C):
+        gather[0, k].wait_send()
+        gather[1, k].start()
+        sent.append(gather[1, k])
 
     def product(matrix, block):
         high, low = split(block)
@@ -160,79 +166,66 @@
     grad_pre = cot_ref[...] * gate * (1.0 + before * (1.0 - gate))
     g = split(grad_pre)
 
-    scatters = []
-    for h in range(2):
+    order = list(range(1, C)) + [0]
+
+    def message_half(h):
         m = mm3(g, (w[0][h * half:(h + 1) * half], w[1][h * half:(h + 1) * half]), ((1,), (1,)))
-        high, low = split(m)
-        both = jnp.concatenate([high, low], axis=1)
-
-        def back(q):
-            x = mm(adj_t[q], both)
-            return x[:, :half] + x[:, half:]
-
-        order = list(range(1, C)) + [0]
+        return jnp.concatenate(split(m), axis=1)
+
+    def back(both, q):
+        x = mm(adj_t[q], both)
+        return x[:, :half] + x[:, half:]
+
+    def pair_half(h, both):
         pairs = {}
         for k in order:
-            psend[h, k] = back(chip_at(k) * 2 + other)
+            psend[h, k] = back(both, chip_at(k) * 2 + other)
             pairs[k] = send(psend.at[h, k], precv.at[h, k], p_s.at[h, k], p_r.at[h, k], dom=partner)
-        chips = []
+        return pairs
+
+    def chip_half(h, both, pairs, earlier):
+        copies = []
         for k in order:
-            x = back(chip_at(k) * 2 + core)
+            x = back(both, chip_at(k) * 2 + core)
             pairs[k].wait_recv()
             csend[h, k] = x + precv[h, k]
             if k:
-                chips.append(
-                    send(csend.at[h, k], crecv.at[h, k], c_s.at[h, k], c_r.at[h, k], dom=chip_at(k) * 2 + core)
-                )
-        scatters.append(chips)
-
-        if h == 0:
-            for b in range(2):
-                term = mm3(sums[b], g, ((0,), (0,)))
-                count = half // piece
-                wterm[pl.ds(b * count, count)] = term.reshape(count, piece, feat)
-            bias_term = jnp.broadcast_to(jnp.sum(grad_pre, axis=0, keepdims=True), (8, feat))
-            for o in range(K):
-                w1s[o, pl.ds(0, piece)] = wterm[r * K + o]
-                w1s[o, pl.ds(piece, 8)] = bias_term
-            ones = []
-            for k in range(1, D):
-                owner = dom_at(k)
-                if K == D:
-                    ones.append(send(w1s.at[owner], w1r.at[k], w1_s.at[k], w1_r.at[k], dom=owner))
-                else:
-                    owner_in = jnp.minimum(owner, K - 1)
-                    c = copy(w1s.at[owner_in], w1r.at[k], w1_s.at[k], w1_r.at[k], dom=owner)
-                    ones.append(c)
-
-                    @pl.when(owner < K)
-                    def _(c=c):
-                        c.start()
-                        c.wait_send()
-
-    twos = [
-        copy(w2b.at[jnp.minimum(d, K - 1)], w2b.at[jnp.minimum(d, K - 1)], w2_s.at[k], w2_r.at[k], dom=dom_at(k))
+                c = copy(csend.at[h, k], crecv.at[h, k], c_s.at[h, k], c_r.at[h, k], dom=chip_at(k) * 2 + core)
+                if earlier is not None:
+                    earlier[k - 1].wait_send()
+                c.start()
+                copies.append(c)
+        return copies
+
+    scatters = []
+    both = message_half(0)
+    pairs = pair_half(0, both)
+    scatters.append(chip_half(0, both, pairs, None))
+    both = message_half(1)
+    pairs = pair_half(1, both)
+
+    for b in range(2):
+        term = mm3(sums[b], g, ((0,), (0,)))
+        count = half // piece
+        wterm[pl.ds(b * count, count)] = term.reshape(count, piece, feat)
+    bias_term = jnp.broadcast_to(jnp.sum(grad_pre, axis=0, keepdims=True), (8, feat))
+    for o in range(K):
+        w1s[o, pl.ds(0, piece)] = wterm[r * K + o]
+        w1s[o, pl.ds(piece, 8)] = bias_term
+    ones = [
+        send(w1s.at[jnp.minimum(dom_at(k), K - 1)], w1r.at[k], w1_s.at[k], w1_r.at[k], dom=dom_at(k))
         for k in range(1, D)
     ]
-
-    def own_piece():
-        total = w1s[jnp.minimum(d, K - 1)]
-        for k in range(1, D):
-            ones[k - 1].wait_recv()
-            total = total + w1r[k]
-        w2b[jnp.minimum(d, K - 1)] = total
-        for c in twos:
-            c.start()
-
-    if K == D:
-        own_piece()
-        sent.extend(twos)
-    else:
-        @pl.when(d < K)
-        def _():
-            own_piece()
-            for c in twos:
-                c.wait_send()
+    scatters.append(chip_half(1, both, pairs, scatters[0]))
+    sent.extend(scatters[1])
+
+    total = w1s[jnp.minimum(d, K - 1)]
+    for k in range(1, D):
+        ones[k - 1].wait_recv()
+        total = total + w1r[k]
+    gbias_ref[...] = total[piece:piece + 1]
+    w2b[r] = total[:piece]
+    twos = [send(w2b.at[r], w2b.at[r], w2_s.at[k], w2_r.at[k], rep=rep_at(k)) for k in range(1, R)]
 
     def back_sum(h):
         total = csend[h, 0]
@@ -244,25 +237,55 @@
 
     first = back_sum(0)
 
-    for k in range(1, D):
-        source = lax.rem(d + D - k, D)
+    for c in twos:
+        c.wait_recv()
+
+    def when_owner(place, action):
         if K == D:
-            copy(w2b.at[source], w2b.at[source], w2_s.at[k], w2_r.at[k], dom=dom_at(k)).wait_recv()
+            action()
         else:
-            @pl.when(source < K)
-            def _(k=k, source=source):
-                s = jnp.minimum(source, K - 1)
-                copy(w2b.at[s], w2b.at[s], w2_s.at[k], w2_r.at[k], dom=dom_at(k)).wait_recv()
-    w3b[r] = w2b[:, :piece].reshape(K * piece, feat)
-    threes = [send(w3b.at[r], w3b.at[r], w3_s.at[k], w3_r.at[k], rep=rep_at(k)) for k in range(1, R)]
-    gbias_ref[...] = w2b[0, piece:piece + 1]
-
+            pl.when(place < K // 2)(action)
+
+    def three(k, source):
+        slot = jnp.minimum(source, K // 2 - 1) * 2 + core
+        return copy(w3b.at[slot], w3b.at[slot], w3_s.at[k], w3_r.at[k], dom=chip_at(k) * 2 + core)
+
+    def four(k, side):
+        source = lax.rem(chip + C - k, C)
+        slot = jnp.minimum(source, K // 2 - 1) * 2 + side
+        return copy(w3b.at[slot], w3b.at[slot], w4_s.at[k], w4_r.at[k], dom=partner)
+
+    def hand_out():
+        w3b[jnp.minimum(chip, K // 2 - 1) * 2 + core] = w2b[...]
+        for k in range(1, C):
+            three(k, chip).start()
+        four(0, core).start()
+
+    when_owner(chip, hand_out)
     ends = [rep_gather(0, first, srcp, rs2, gbuf, e_s, e_r)]
     second = back_sum(1)
+    for k in range(1, C):
+        def pass_on(k=k):
+            three(k, lax.rem(chip + C - k, C)).wait_recv()
+            four(k, core).start()
+
+        when_owner(lax.rem(chip + C - k, C), pass_on)
     ends.append(rep_gather(1, second, srcp, rs2, gbuf, e_s, e_r))
-    for c in threes:
-        c.wait_recv()
-    gweight_ref[...] = w3b[...].reshape(feat, feat)
+    for k in range(C):
+        def take(k=k):
+            four(k, other).wait_recv()
+            four(k, core).wait_send()
+
+        when_owner(lax.rem(chip + C - k, C), take)
+
+    def handed():
+        for k in range(1, C):
+            three(k, chip).wait_send()
+
+    when_owner(chip, handed)
+    for b in range(R):
+        for o in range(K):
+            gweight_ref[pl.ds((b * K + o) * piece, piece)] = w3b[o, b]
     for h in range(2):
         for c in ends[h]:
             c.wait_recv()
@@ -305,8 +328,8 @@
             pltpu.VMEM((R * K, piece, feat), F32),
             pltpu.VMEM((K, piece + 8, feat), F32),
             pltpu.VMEM((D, piece + 8, feat), F32),
-            pltpu.VMEM((K, piece + 8, feat), F32),
-            pltpu.VMEM((R, share, feat), F32),
+            pltpu.VMEM((R, piece, feat), F32),
+            pltpu.VMEM((K, R, piece, feat), F32),
             pltpu.VMEM((2, C, n_rows, half), F32),
             pltpu.VMEM((2, C, n_rows, half), F32),
             pltpu.VMEM((2, C, n_rows, half), F32),
@@ -319,8 +342,9 @@
         + [sems(2, R)] * 4
         + [sems(2, C)] * 4
         + [sems(2, R)] * 4
-        + [sems(D)] * 4
-        + [sems(R)] * 2,
+        + [sems(D)] * 2
+        + [sems(R)] * 2
+        + [sems(C)] * 4,
         compiler_params=pltpu.CompilerParams(
             collective_id=0, has_side_effects=True, vmem_limit_bytes=56 * 1024 * 1024
         ),

time: 76.2 us -> 69 us (0.906)
  Pallas kernels: 71.4 us -> 64.1 us
    pallas_call x1, Pallas kernels: 71.4 us -> 64.1 us  [body(): pl.pallas_call(functools.partial(kernel, D, R, K), out_shape=(jax.ShapeDt...]
where the time goes in v2:
time: 69 us; the launch traced here: 68.8 us
  Pallas kernels  64.1 us (93%)
  local copies, waits for them, and re-layouts  4.03 us (6%)
    pallas_call x1, Pallas kernels, body(): pl.pallas_call(functools.partial(kernel, D, R, K), out_shape=(jax.ShapeDt...  64.1 us
    unnamed x10, local copies, waits for them, and re-layouts  4.03 us

profile of v2, /device:TPU:0, one launch (start us, length us, event | category | flops | bytes accessed | tf_op | source)
XLA Modules:
  0.0 68.8 jit_solution(17659312822088772280)
XLA Ops:
  0.6 64.1 %layer.1 = (f32[256,256]{1,0:T(8,128)}, f32[256,256]{1,0:T(8,128)}, f32[256,256]{1,0:T(8,128)}, f32[1,256]{1,0:T(1,128)}) custom-call(s32[1,16]{1,0:T(1,128)} %rows_ref.1, s32[1,16]{1,0:T(1,128)} %cols_ref.1, f32[256,256]{1,0:T(8,128)} %feat_ref.1, bf16[1,16,128,128]{3,2,1,0:T(8,128)(2,1)} %tiles_ref.1, f32[256,256]{1,0:T(8,128)} %weight_ref.1, ...), custom_call_target="tpu_custom_call" | custom-call | tf_op jit(solution)/shard_map/layer/pallas_call | solution.py:311
  64.8 0.0 copy-start.1
  64.8 1.7 %copy.15 = f32[256,256]{1,0:T(8,128)} copy(f32[256,256]{1,0:T(8,128)} %get-tuple-element.16) | data formatting | bytes 524288
  66.5 0.0 copy-done.1
  66.5 0.0 copy-start
  66.5 0.7 %copy.16 = f32[256,256]{1,0:T(8,128)} copy(f32[256,256]{1,0:T(8,128)S(1)} %copy-done.1) | data formatting | bytes 524288
  67.2 0.3 copy-done
  67.5 0.0 copy-start.2
  67.5 0.7 %copy.17 = f32[256,256]{1,0:T(8,128)} copy(f32[256,256]{1,0:T(8,128)S(1)} %copy-done) | data formatting | bytes 524288
  68.2 0.0 copy-done.2
  68.2 0.6 copy.18
Async XLA Ops:
  64.8 1.7 %copy-start.1 = (f32[256,256]{1,0:T(8,128)S(1)}, f32[256,256]{1,0:T(8,128)}, u32[]{:S(2)}) copy-start(f32[256,256]{1,0:T(8,128)} %get-tuple-element.17) | copy-start | bytes 786436
  66.5 1.0 %copy-start = (f32[256,256]{1,0:T(8,128)S(1)}, f32[256,256]{1,0:T(8,128)}, u32[]{:S(2)}) copy-start(f32[256,256]{1,0:T(8,128)} %get-tuple-element.18) | copy-start | bytes 786436
  67.5 0.7 %copy-start.2 = (f32[1,256]{1,0:T(1,128)S(1)}, f32[1,256]{1,0:T(1,128)}, u32[]{:S(2)}) copy-start(f32[1,256]{1,0:T(1,128)} %get-tuple-element.11) | copy-start | bytes 3076

commit v3 on v2

--- a/solution.py
+++ b/solution.py
@@ -144,14 +144,14 @@
             relay[h, k] = send(fbuf.at[h, k, 0], fbuf.at[h, k, 1], l_s.at[h, k], l_r.at[h, k], dom=partner)
             source = lax.rem(chip + C - k, C)
             total = total + product(adj[source * 2 + core], fbuf[h, k, 0])
+        if h:
+            gathers.append(rep_gather(0, reduces[0], part, rsbuf, agg, g_s, g_r))
         for k in range(1, C):
             source = lax.rem(chip + C - k, C)
             relay[h, k].wait_recv()
             total = total + product(adj[source * 2 + other], fbuf[h, k, 1])
         part[h] = total.reshape(R, reduce_rows, half)
         reduces.append(rep_reduce(h, part, rsbuf, b_s, b_r))
-        if h == 0:
-            gathers.append(rep_gather(0, reduces[0], part, rsbuf, agg, g_s, g_r))
     gathers.append(rep_gather(1, reduces[1], part, rsbuf, agg, g_s, g_r))
 
     sums = []
@@ -294,6 +294,11 @@
         c.wait_send()
 
 
+def store(*refs):
+    for source, target in zip(refs[:4], refs[4:]):
+        target[...] = source[...]
+
+
 def body(D, R, features, tile_values, tile_rows, tile_cols, weight, bias, cotangent):
     n_rows, feat = features.shape
     half = feat // 2
@@ -350,6 +355,13 @@
         ),
         name="layer",
     )(tile_rows, tile_cols, features, tile_values, weight, bias.reshape(1, feat), cotangent)
+    out = pl.pallas_call(
+        store,
+        out_shape=tuple(jax.ShapeDtypeStruct(x.shape, F32) for x in out),
+        in_specs=[vmem] * 4,
+        out_specs=(vmem,) * 4,
+        name="store",
+    )(*out)
     activations, grad_features, grad_weight, grad_bias = out
     return activations, grad_features, grad_weight, grad_bias.reshape(feat)
 

time: 69 us -> 66 us (0.957)
  local copies, waits for them, and re-layouts: 4.03 us -> 0 us
  Pallas kernels: 64.1 us -> 65.2 us
    unnamed x10 -> x0, local copies, waits for them, and re-layouts: 4.03 us -> none
    pallas_call x0 -> x1, Pallas kernels: none -> 2.01 us  [body(): pl.pallas_call(store, out_shape=tuple((jax.ShapeDtypeStruct(x.shape, F32)...]
    pallas_call x1, Pallas kernels: 64.1 us -> 63.2 us  [body(): pl.pallas_call(functools.partial(kernel, D, R, K), out_shape=(jax.ShapeDt...]
where the time goes in v3:
time: 66 us; the launch traced here: 65.8 us
  Pallas kernels  65.2 us (99%)
    pallas_call x1, Pallas kernels, body(): pl.pallas_call(functools.partial(kernel, D, R, K), out_shape=(jax.ShapeDt...  63.2 us
    pallas_call x1, Pallas kernels, body(): pl.pallas_call(store, out_shape=tuple((jax.ShapeDtypeStruct(x.shape, F32)...  2.01 us

profile of v3, /device:TPU:0, one launch (start us, length us, event | category | flops | bytes accessed | tf_op | source)
XLA Modules:
  0.0 65.8 jit_solution(14428038407866162244)
XLA Ops:
  0.6 63.2 %layer.1 = (f32[256,256]{1,0:T(8,128)}, f32[256,256]{1,0:T(8,128)}, f32[256,256]{1,0:T(8,128)}, f32[1,256]{1,0:T(1,128)}) custom-call(s32[1,16]{1,0:T(1,128)} %rows_ref.1, s32[1,16]{1,0:T(1,128)} %cols_ref.1, f32[256,256]{1,0:T(8,128)} %feat_ref.1, bf16[1,16,128,128]{3,2,1,0:T(8,128)(2,1)} %tiles_ref.1, f32[256,256]{1,0:T(8,128)} %weight_ref.1, ...), custom_call_target="tpu_custom_call" | custom-call | tf_op jit(solution)/shard_map/layer/pallas_call | solution.py:316
  63.8 2.0 %store.1 = (f32[256,256]{1,0:T(8,128)}, f32[256,256]{1,0:T(8,128)}, f32[256,256]{1,0:T(8,128)}, f32[1,256]{1,0:T(1,128)}) custom-call(f32[256,256]{1,0:T(8,128)} %get-tuple-element.12.refs_0_, f32[256,256]{1,0:T(8,128)} %get-tuple-element.13.refs_1_, f32[256,256]{1,0:T(8,128)} %get-tuple-element.14.refs_2_, f32[1,256]{1,0:T(1,128)} %get-tuple-element.15.refs_3_), custom_call_target="tpu_custom_call" | custom-call | tf_op jit(solution)/shard_map/store/pallas_call | solution.py:358

commit v4 on v3

--- a/solution.py
+++ b/solution.py
@@ -26,9 +26,9 @@
 
 def kernel(
     D, R, K,
-    rows_ref, cols_ref, feat_ref, tiles_ref, weight_ref, bias_ref, cot_ref,
+    rows_ref, cols_ref, feat_ref, tiles_hbm, weight_hbm, bias_ref, cot_hbm,
     act_ref, gfeat_ref, gweight_ref, gbias_ref,
-    adj, adj_t, fbuf, part, rsbuf, agg, wterm, w1s, w1r, w2b, w3b,
+    tiles_ref, weight_ref, cot_ref, in_s, adj, adj_t, fbuf, part, rsbuf, agg, wterm, w1s, w1r, w2b, w3b,
     psend, precv, csend, crecv, srcp, rs2, gbuf,
     a_s, a_r, l_s, l_r, b_s, b_r, g_s, g_r,
     p_s, p_r, c_s, c_r, d_s, d_r, e_s, e_r,
@@ -71,11 +71,17 @@
         sent.append(c)
         return c
 
+    loads = [
+        pltpu.make_async_copy(a, b, in_s.at[i])
+        for i, (a, b) in enumerate(((tiles_hbm, tiles_ref), (weight_hbm, weight_ref), (cot_hbm, cot_ref)))
+    ]
     barrier = pltpu.get_barrier_semaphore()
     for k in range(1, D):
         pl.semaphore_signal(barrier, inc=1, device_id={"dom": dom_at(k), "rep": r}, device_id_type=pl.DeviceIdType.MESH)
     for k in range(1, R):
         pl.semaphore_signal(barrier, inc=1, device_id={"dom": d, "rep": rep_at(k)}, device_id_type=pl.DeviceIdType.MESH)
+    for c in loads:
+        c.start()
     pl.semaphore_wait(barrier, D - 1 + R - 1)
 
     lanes = [pl.ds(h * half, half) for h in range(2)]
@@ -104,6 +110,8 @@
                 adj_t[q, pl.ds(j * tile, tile), pl.ds(b * tile, tile)] = (turned * keep).astype(BF16)
         return carry
 
+    for c in loads:
+        c.wait()
     lax.fori_loop(0, D, place, 0)
     w = split(weight_ref[...])
     for k in range(1, C):
@@ -219,6 +227,16 @@
     scatters.append(chip_half(1, both, pairs, scatters[0]))
     sent.extend(scatters[1])
 
+    def back_sum(h):
+        total = csend[h, 0]
+        for k in range(1, C):
+            scatters[h][k - 1].wait_recv()
+            total = total + crecv[h, k]
+        srcp[h] = total.reshape(R, reduce_rows, half)
+        return rep_reduce(h, srcp, rs2, d_s, d_r)
+
+    first = back_sum(0)
+
     total = w1s[jnp.minimum(d, K - 1)]
     for k in range(1, D):
         ones[k - 1].wait_recv()
@@ -226,16 +244,6 @@
     gbias_ref[...] = total[piece:piece + 1]
     w2b[r] = total[:piece]
     twos = [send(w2b.at[r], w2b.at[r], w2_s.at[k], w2_r.at[k], rep=rep_at(k)) for k in range(1, R)]
-
-    def back_sum(h):
-        total = csend[h, 0]
-        for k in range(1, C):
-            scatters[h][k - 1].wait_recv()
-            total = total + crecv[h, k]
-        srcp[h] = total.reshape(R, reduce_rows, half)
-        return rep_reduce(h, srcp, rs2, d_s, d_r)
-
-    first = back_sum(0)
 
     for c in twos:
         c.wait_recv()
@@ -308,6 +316,7 @@
     piece = share // K
     chunk = n_rows // R
     vmem = pl.BlockSpec(memory_space=pltpu.VMEM)
+    anywhere = pl.BlockSpec(memory_space=pl.ANY)
     smem = pl.BlockSpec(memory_space=pltpu.SMEM)
 
     def sems(*shape):
@@ -321,9 +330,13 @@
             jax.ShapeDtypeStruct((feat, feat), F32),
             jax.ShapeDtypeStruct((1, feat), F32),
         ),
-        in_specs=[smem, smem] + [vmem] * 5,
+        in_specs=[smem, smem, vmem, anywhere, anywhere, vmem, anywhere],
         out_specs=(vmem,) * 4,
         scratch_shapes=[
+            pltpu.VMEM(tile_values.shape, BF16),
+            pltpu.VMEM(weight.shape, F32),
+            pltpu.VMEM(cotangent.shape, F32),
+            sems(3),
             pltpu.VMEM((D, n_rows, n_rows), BF16),
             pltpu.VMEM((D, n_rows, n_rows), BF16),
             pltpu.VMEM((2, C, 2, n_rows, half), F32),

time: 66 us -> 64.8 us (0.982)
  Pallas kernels: 65.2 us -> 64 us
    pallas_call x1, Pallas kernels: 63.2 us -> 62 us  [body(): pl.pallas_call(functools.partial(kernel, D, R, K), out_shape=(jax.ShapeDt...]
where the time goes in v4:
time: 64.8 us; the launch traced here: 64.6 us
  Pallas kernels  64 us (99%)
    pallas_call x1, Pallas kernels, body(): pl.pallas_call(functools.partial(kernel, D, R, K), out_shape=(jax.ShapeDt...  62 us
    pallas_call x1, Pallas kernels, body(): pl.pallas_call(store, out_shape=tuple((jax.ShapeDtypeStruct(x.shape, F32)...  2.01 us

profile of v4, /device:TPU:0, one launch (start us, length us, event | category | flops | bytes accessed | tf_op | source)
XLA Modules:
  0.0 64.6 jit_solution(5453656348357790641)
XLA Ops:
  0.6 62.0 %layer.1 = (f32[256,256]{1,0:T(8,128)}, f32[256,256]{1,0:T(8,128)}, f32[256,256]{1,0:T(8,128)}, f32[1,256]{1,0:T(1,128)}) custom-call(s32[1,16]{1,0:T(1,128)} %rows_ref.1, s32[1,16]{1,0:T(1,128)} %cols_ref.1, f32[256,256]{1,0:T(8,128)} %feat_ref.1, bf16[1,16,128,128]{3,2,1,0:T(8,128)(2,1)} %tiles_hbm.1, f32[256,256]{1,0:T(8,128)} %weight_hbm.1, ...), custom_call_target="tpu_custom_call" | custom-call | tf_op jit(solution)/shard_map/layer/pallas_call | solution.py:325
  62.6 2.0 %store.1 = (f32[256,256]{1,0:T(8,128)}, f32[256,256]{1,0:T(8,128)}, f32[256,256]{1,0:T(8,128)}, f32[1,256]{1,0:T(1,128)}) custom-call(f32[256,256]{1,0:T(8,128)} %get-tuple-element.12.refs_0_, f32[256,256]{1,0:T(8,128)} %get-tuple-element.13.refs_1_, f32[256,256]{1,0:T(8,128)} %get-tuple-element.14.refs_2_, f32[1,256]{1,0:T(1,128)} %get-tuple-element.15.refs_3_), custom_call_target="tpu_custom_call" | custom-call | tf_op jit(solution)/shard_map/store/pallas_call | solution.py:371
